TPU v7x, 32 devices: a whole 2x2x4 slice. The times are simulated.
32 devices in a mesh: ctx: 8 (over z, x), dec: 4 (over y, core).
Axes of the slice: x: 2, y: 2, z: 4, core: 2. Of those that a mesh axis runs over, the one named last changes fastest.
Arguments:
- queries: bfloat16 [64, 2, 8192], P(('ctx', 'dec')), may hold values from -256 to 256
- prompt_keys: bfloat16 [16384, 8, 128], P('ctx', 'dec'), may hold values from -40 to 40
- prompt_values: bfloat16 [16384, 8, 128], P('ctx', 'dec'), may hold values from -6 to 6
- suffix_keys: bfloat16 [64, 1024, 8, 128], P(('ctx', 'dec')), may hold values from -22 to 22
- suffix_values: bfloat16 [64, 1024, 8, 128], P(('ctx', 'dec')), may hold values from -6 to 6
- new_keys: bfloat16 [64, 2, 8, 128], P(('ctx', 'dec')), may hold values from -36 to 36
- new_values: bfloat16 [64, 2, 8, 128], P(('ctx', 'dec')), may hold values from -6 to 6
- lengths: int32 [64], P(('ctx', 'dec')), may hold values from 1 to 1024, as said below
Outputs:
- attended: bfloat16 [64, 2, 8192], P(('ctx', 'dec'))
Inputs may be any that keep to these rules, and one draw needn't show every extreme that they name: `lengths`: at least one sample has exactly 1024 cached suffix tokens in every draw.
All inputs are finite; a program needn't handle non-finite values.
Results may differ from a plain program's by a relative error of at most 0.003.
Values may be sent and summed in bfloat16 or wider, within the bound.
A program may use at most 128 MiB of HBM per device.

v0:
```python
import jax
import jax.numpy as jnp
from jax import lax
from jax.sharding import PartitionSpec as P

MASKED_SCORE = -1e30


def block_part(scores, visible, values, form):
    masked = jnp.where(visible, scores, MASKED_SCORE)
    block_max = jnp.max(masked, axis=-1)
    weights = jnp.where(visible, jnp.exp(masked - block_max[..., None]), 0.0).astype(jnp.bfloat16)
    block_total = jnp.sum(weights, axis=-1, dtype=jnp.float32)
    block_sum = jnp.einsum(form, weights, values, preferred_element_type=jnp.float32)
    return (block_max, block_total, block_sum)


def merge_parts(left, right):
    highest = jnp.maximum(left[0], right[0])
    left_factor = jnp.exp(left[0] - highest)
    right_factor = jnp.exp(right[0] - highest)
    return (
        highest,
        left[1] * left_factor + right[1] * right_factor,
        left[2] * left_factor[..., None] + right[2] * right_factor[..., None],
    )


def combine_leading(moved):
    highest = jnp.max(moved[0], axis=0)
    factors = jnp.exp(moved[0] - highest[None])
    return (
        highest,
        jnp.sum(moved[1] * factors, axis=0),
        jnp.sum(moved[2] * factors[..., None], axis=0),
    )


def empty_state(state_shape, head_dim):
    return (
        jnp.full(state_shape, MASKED_SCORE, jnp.float32),
        jnp.zeros(state_shape, jnp.float32),
        jnp.zeros(state_shape + (head_dim,), jnp.float32),
    )


def prompt_part(rows, prompt_keys, prompt_values):
    row_count, step_count, groups, packed = rows.shape
    positions_here, _, head_dim = prompt_keys.shape
    grouped = rows.reshape(row_count, step_count, groups, packed // head_dim, head_dim)
    key_span = min(512, positions_here)
    key_blocks = prompt_keys.reshape(positions_here // key_span, key_span, groups, head_dim)
    value_blocks = prompt_values.reshape(positions_here // key_span, key_span, groups, head_dim)
    inverse_root = head_dim ** (-0.5)

    def prompt_step(carried, blocks_pair):
        scores = (
            jnp.einsum(
                "rtgqd,kgd->rtgqk", grouped, blocks_pair[0], preferred_element_type=jnp.float32
            )
            * inverse_root
        )
        return (
            merge_parts(carried, block_part(scores, True, blocks_pair[1], "rtgqk,kgd->rtgqd")),
            None,
        )

    initial = empty_state((row_count, step_count, groups, packed // head_dim), head_dim)
    result, _ = lax.scan(prompt_step, initial, (key_blocks, value_blocks))
    return result


def local(
    queries, prompt_keys, prompt_values, suffix_keys, suffix_values, new_keys, new_values, lengths
):
    own_rows, step_count, feature_width = queries.shape
    suffix_length, kv_heads, head_dim = (
        suffix_keys.shape[1],
        suffix_keys.shape[2],
        suffix_keys.shape[3],
    )
    per_group = feature_width // (kv_heads * head_dim)
    by_group = queries.reshape(own_rows, step_count, kv_heads, per_group * head_dim)
    local_rows = lax.all_to_all(by_group, "dec", split_axis=2, concat_axis=0, tiled=True)
    found = prompt_part(
        lax.all_gather(local_rows, "ctx", axis=0, tiled=True), prompt_keys, prompt_values
    )
    grouped = queries.reshape(own_rows, step_count, kv_heads, per_group, head_dim)
    inverse_root = head_dim ** (-0.5)
    suffix_span = min(512, suffix_length)

    def suffix_step(number, carried):
        offset = number * suffix_span
        keys_here = lax.dynamic_slice_in_dim(suffix_keys, offset, suffix_span, 1)
        values_here = lax.dynamic_slice_in_dim(suffix_values, offset, suffix_span, 1)
        scores = (
            jnp.einsum("stgqd,skgd->stgqk", grouped, keys_here, preferred_element_type=jnp.float32)
            * inverse_root
        )
        positions = offset + jnp.arange(suffix_span, dtype=jnp.int32)
        visible = (positions[None, :] < lengths[:, None])[:, None, None, None, :]
        return merge_parts(carried, block_part(scores, visible, values_here, "stgqk,skgd->stgqd"))

    own_initial = empty_state((own_rows, step_count, kv_heads, per_group), head_dim)
    suffix_state = lax.fori_loop(0, suffix_length // suffix_span, suffix_step, own_initial)
    scores = (
        jnp.einsum("stgqd,sugd->stgqu", grouped, new_keys, preferred_element_type=jnp.float32)
        * inverse_root
    )
    step_index = jnp.arange(step_count, dtype=jnp.int32)
    visible = (step_index[None, :] <= step_index[:, None])[None, :, None, None, :]
    suffix_state = merge_parts(
        suffix_state, block_part(scores, visible, new_values, "stgqu,sugd->stgqd")
    )
    moved = (
        lax.all_to_all(found[0][None], "ctx", split_axis=1, concat_axis=0, tiled=True),
        lax.all_to_all(found[1][None], "ctx", split_axis=1, concat_axis=0, tiled=True),
        lax.all_to_all(found[2][None], "ctx", split_axis=1, concat_axis=0, tiled=True),
    )
    mine = combine_leading(moved)
    prompt_mine = (
        lax.all_to_all(mine[0], "dec", split_axis=0, concat_axis=2, tiled=True),
        lax.all_to_all(mine[1], "dec", split_axis=0, concat_axis=2, tiled=True),
        lax.all_to_all(mine[2], "dec", split_axis=0, concat_axis=2, tiled=True),
    )
    combined = merge_parts(prompt_mine, suffix_state)
    attended = combined[2] / combined[1][..., None]
    return attended.astype(jnp.bfloat16).reshape(own_rows, step_count, feature_width)


def solution(mesh):
    return jax.shard_map(
        local,
        mesh=mesh,
        in_specs=(
            P(("ctx", "dec"), None, None),
            P("ctx", "dec", None),
            P("ctx", "dec", None),
            P(("ctx", "dec"), None, None, None),
            P(("ctx", "dec"), None, None, None),
            P(("ctx", "dec"), None, None, None),
            P(("ctx", "dec"), None, None, None),
            P(("ctx", "dec")),
        ),
        out_specs=P(("ctx", "dec"), None, None),
        check_vma=False,
    )
```

profile of v0, /device:TPU:0, one launch (start us, length us, event | category | flops | bytes accessed | tf_op | source)
XLA Modules:
  0.0 157.7 jit_solution(12430609175065005582)
XLA Ops:
  0.0 1.5 copy.230
  1.5 4.2 %all-to-all-start = ((bf16[2,2,8,1024]{3,1,0,2:T(2,128)(2,1)}), bf16[2,2,8,1024]{3,1,0,2:T(2,128)(2,1)S(1)}, u32[]{:S(2)}, u32[]{:S(2)}) async-start(bf16[2,2,8,1024]{3,1,0,2:T(2,128)(2,1)} %bitcast.126), calls=%async_computation | async-start | bytes 131072 | tf_op jit(solution)/shard_map/all_to_all | solution.py:84
  5.8 4.1 %all-to-all-done = bf16[2,2,8,1024]{3,1,0,2:T(2,128)(2,1)S(1)} async-done(((bf16[2,2,8,1024]{3,1,0,2:T(2,128)(2,1)}), bf16[2,2,8,1024]{3,1,0,2:T(2,128)(2,1)S(1)}, u32[]{:S(2)}, u32[]{:S(2)}) %all-to-all-start) | async-done | bytes 65568 | tf_op jit(solution)/shard_map/all_to_all | solution.py:84
  9.9 32.3 %all_gather.3 = bf16[64,2,2,1024]{3,2,1,0:T(2,128)(2,1)S(1)} all-gather(bf16[8,2,2,1024]{3,2,1,0:T(2,128)(2,1)S(1)} %bitcast.156), channel_id=1, replica_groups=mesh['ctx'=8,'dec'=4] {'ctx'}, dimensions={0}, use_global_device_ids=true | all-gather | bytes 589824 | tf_op jit(solution)/shard_map/all_gather | solution.py:86
  42.2 0.3 reshape.105
  42.5 0.2 copy.130
  42.8 34.3 %while.33 = (s32[]{:T(128)}, f32[64,2,2,8]{0,3,1,2:T(8,128)S(1)}, f32[64,2,2,8]{0,3,1,2:T(8,128)S(1)}, f32[64,2,2,8,128]{4,0,3,1,2:T(8,128)S(1)}, bf16[4,512,2,1...) while((s32[]{:T(128)}, f32[64,2,2,8]{0,3,1,2:T(8,128)S(1)}, ...), condition=%wide.region_3.4_spmd.clone, body=%wide.region_0.3_spmd.clone.sunk | while | flops 548417536 | bytes 33669256 | solution.py:69
  42.8 1.4 constant_dynamic-slice_fusion.6
  44.2 0.8 bitcast_reduce_fusion.2
  45.0 1.9 %copy-done.1 = f32[2,512,64,2,8]{1,2,4,3,0:T(8,128)} copy-done((f32[2,512,64,2,8]{1,2,4,3,0:T(8,128)}, f32[2,512,64,2,8]{1,2,4,3,0:T(8,128)S(1)}, u32[]{:S(2)}) %copy-start.1) | copy-done | bytes 4194328 | tf_op jit(solution)/shard_map/while
  46.9 1.3 convert_reduce_fusion.5
  48.2 3.1 %fusion.53 = f32[64,2,2,8,128]{4,0,3,1,2:T(8,128)S(1)} fusion(f32[64,2,2,8,128]{4,0,3,1,2:T(8,128)S(1)} %get-tuple-element.554, f32[64,2,2,8]{0,3,1,2:T(8,128)S(1)} %get-tuple-element.487, f32[64,2,2,8]{0,3,1,2:T(8,128)S(1)} %get-tuple-element.488, pred[]{:T(512)S(6)} %compare.6, f32[2,512,64,2,8]{1,2,4,3,0:T(8,128)} %copy-done.1, ...), kind=kOutput, calls=%fused_computation.7.clone.1 | convolution fusion | flops 272629760 | bytes 6578177 | tf_op jit(solution)/shard_map/while/body/eval_jaxpr/rtgqk,kgd->rtgqd/dot_general | solution.py:14
  51.4 1.4 constant_dynamic-slice_fusion.6
  52.8 0.8 bitcast_reduce_fusion.2
  53.6 1.9 %copy-done.1 = f32[2,512,64,2,8]{1,2,4,3,0:T(8,128)} copy-done((f32[2,512,64,2,8]{1,2,4,3,0:T(8,128)}, f32[2,512,64,2,8]{1,2,4,3,0:T(8,128)S(1)}, u32[]{:S(2)}) %copy-start.1) | copy-done | bytes 4194328 | tf_op jit(solution)/shard_map/while
  55.5 1.3 convert_reduce_fusion.5
  56.8 3.1 %fusion.53 = f32[64,2,2,8,128]{4,0,3,1,2:T(8,128)S(1)} fusion(f32[64,2,2,8,128]{4,0,3,1,2:T(8,128)S(1)} %get-tuple-element.554, f32[64,2,2,8]{0,3,1,2:T(8,128)S(1)} %get-tuple-element.487, f32[64,2,2,8]{0,3,1,2:T(8,128)S(1)} %get-tuple-element.488, pred[]{:T(512)S(6)} %compare.6, f32[2,512,64,2,8]{1,2,4,3,0:T(8,128)} %copy-done.1, ...), kind=kOutput, calls=%fused_computation.7.clone.1 | convolution fusion | flops 272629760 | bytes 6578177 | tf_op jit(solution)/shard_map/while/body/eval_jaxpr/rtgqk,kgd->rtgqd/dot_general | solution.py:14
  59.9 1.4 constant_dynamic-slice_fusion.6
  61.3 0.8 bitcast_reduce_fusion.2
  62.1 1.9 %copy-done.1 = f32[2,512,64,2,8]{1,2,4,3,0:T(8,128)} copy-done((f32[2,512,64,2,8]{1,2,4,3,0:T(8,128)}, f32[2,512,64,2,8]{1,2,4,3,0:T(8,128)S(1)}, u32[]{:S(2)}) %copy-start.1) | copy-done | bytes 4194328 | tf_op jit(solution)/shard_map/while
  64.0 1.3 convert_reduce_fusion.5
  65.4 3.1 %fusion.53 = f32[64,2,2,8,128]{4,0,3,1,2:T(8,128)S(1)} fusion(f32[64,2,2,8,128]{4,0,3,1,2:T(8,128)S(1)} %get-tuple-element.554, f32[64,2,2,8]{0,3,1,2:T(8,128)S(1)} %get-tuple-element.487, f32[64,2,2,8]{0,3,1,2:T(8,128)S(1)} %get-tuple-element.488, pred[]{:T(512)S(6)} %compare.6, f32[2,512,64,2,8]{1,2,4,3,0:T(8,128)} %copy-done.1, ...), kind=kOutput, calls=%fused_computation.7.clone.1 | convolution fusion | flops 272629760 | bytes 6578177 | tf_op jit(solution)/shard_map/while/body/eval_jaxpr/rtgqk,kgd->rtgqd/dot_general | solution.py:14
  68.5 1.4 constant_dynamic-slice_fusion.6
  69.9 0.8 bitcast_reduce_fusion.2
  70.7 1.9 %copy-done.1 = f32[2,512,64,2,8]{1,2,4,3,0:T(8,128)} copy-done((f32[2,512,64,2,8]{1,2,4,3,0:T(8,128)}, f32[2,512,64,2,8]{1,2,4,3,0:T(8,128)S(1)}, u32[]{:S(2)}) %copy-start.1) | copy-done | bytes 4194328 | tf_op jit(solution)/shard_map/while
  72.6 1.3 convert_reduce_fusion.5
  73.9 3.1 %fusion.53 = f32[64,2,2,8,128]{4,0,3,1,2:T(8,128)S(1)} fusion(f32[64,2,2,8,128]{4,0,3,1,2:T(8,128)S(1)} %get-tuple-element.554, f32[64,2,2,8]{0,3,1,2:T(8,128)S(1)} %get-tuple-element.487, f32[64,2,2,8]{0,3,1,2:T(8,128)S(1)} %get-tuple-element.488, pred[]{:T(512)S(6)} %compare.6, f32[2,512,64,2,8]{1,2,4,3,0:T(8,128)} %copy-done.1, ...), kind=kOutput, calls=%fused_computation.7.clone.1 | convolution fusion | flops 272629760 | bytes 6578177 | tf_op jit(solution)/shard_map/while/body/eval_jaxpr/rtgqk,kgd->rtgqd/dot_general | solution.py:14
  77.1 0.1 copy.133
  77.2 0.8 reshape.106
  78.0 5.6 %all-to-all-start.2 = ((f32[8,1,256]{2,1,0:T(1,128)}), f32[8,1,256]{2,1,0:T(1,128)S(1)}, u32[]{:S(2)}, u32[]{:S(2)}) async-start(f32[8,1,256]{2,1,0:T(1,128)} %reshape.106), calls=%async_computation.2 | async-start | bytes 16384 | tf_op jit(solution)/shard_map/all_to_all | solution.py:116
  83.8 0.8 reshape.108
  84.6 5.5 %all-to-all-done.2 = f32[8,1,256]{2,1,0:T(1,128)S(1)} async-done(((f32[8,1,256]{2,1,0:T(1,128)}), f32[8,1,256]{2,1,0:T(1,128)S(1)}, u32[]{:S(2)}, u32[]{:S(2)}) %all-to-all-start.2) | async-done | bytes 8224 | tf_op jit(solution)/shard_map/all_to_all | solution.py:116
  90.1 3.3 %all-to-all-start.5 = ((f32[8,1,256]{2,1,0:T(1,128)}), f32[8,1,256]{2,1,0:T(1,128)S(1)}, u32[]{:S(2)}, u32[]{:S(2)}) async-start(f32[8,1,256]{2,1,0:T(1,128)} %reshape.108), calls=%async_computation.5 | async-start | bytes 16384 | tf_op jit(solution)/shard_map/all_to_all | solution.py:117
  93.6 0.6 broadcast.134
  94.2 0.7 reduce.1
  94.9 0.2 reshape.107
  95.4 4.5 %all-to-all-done.5 = f32[8,1,256]{2,1,0:T(1,128)S(1)} async-done(((f32[8,1,256]{2,1,0:T(1,128)}), f32[8,1,256]{2,1,0:T(1,128)S(1)}, u32[]{:S(2)}, u32[]{:S(2)}) %all-to-all-start.5) | async-done | bytes 8224 | tf_op jit(solution)/shard_map/all_to_all | solution.py:117
  99.9 0.7 reduce
  100.6 0.2 reshape.109
  101.1 0.7 copy.153
  101.8 3.3 %all-to-all-start.6 = ((f32[8,2,2,8]{3,2,1,0:T(2,128)}), f32[8,2,2,8]{3,2,1,0:T(2,128)S(1)}, u32[]{:S(2)}, u32[]{:S(2)}) async-start(f32[8,2,2,8]{3,2,1,0:T(2,128)} %copy.153), calls=%async_computation.6 | async-start | bytes 32768 | tf_op jit(solution)/shard_map/all_to_all | solution.py:123
  105.0 0.4 fusion.38
  105.5 0.6 copy.140
  106.1 2.8 %all-to-all-done.6 = f32[8,2,2,8]{3,2,1,0:T(2,128)S(1)} async-done(((f32[8,2,2,8]{3,2,1,0:T(2,128)}), f32[8,2,2,8]{3,2,1,0:T(2,128)S(1)}, u32[]{:S(2)}, u32[]{:S(2)}) %all-to-all-start.6) | async-done | bytes 1056 | tf_op jit(solution)/shard_map/all_to_all | solution.py:123
  108.8 3.2 %all-to-all-start.4 = ((f32[8,2,2,8]{3,2,1,0:T(2,128)}), f32[8,2,2,8]{3,2,1,0:T(2,128)S(1)}, u32[]{:S(2)}, u32[]{:S(2)}) async-start(f32[8,2,2,8]{3,2,1,0:T(2,128)} %copy.140), calls=%async_computation.4 | async-start | bytes 32768 | tf_op jit(solution)/shard_map/all_to_all | solution.py:122
  112.3 1.6 %copy.229 = f32[64,2,2,8,128]{4,3,1,2,0:T(8,128)} copy(f32[64,2,2,8,128]{4,0,3,1,2:T(8,128)S(1)} %get-tuple-element.185) | data formatting | bytes 2097152 | tf_op jit(solution)/shard_map/while | solution.py:69
  113.9 2.0 %all-to-all-done.4 = f32[8,2,2,8]{3,2,1,0:T(2,128)S(1)} async-done(((f32[8,2,2,8]{3,2,1,0:T(2,128)}), f32[8,2,2,8]{3,2,1,0:T(2,128)S(1)}, u32[]{:S(2)}, u32[]{:S(2)}) %all-to-all-start.4) | async-done | bytes 1056 | tf_op jit(solution)/shard_map/all_to_all | solution.py:122
  115.9 4.2 %all-to-all-start.1 = ((f32[1,64,2,2,8,128]{5,4,2,3,0,1:T(8,128)}), f32[1,64,2,2,8,128]{5,4,2,3,0,1:T(8,128)}, u32[]{:S(2)}, u32[]{:S(2)}) async-start(f32[1,64,2,2,8,128]{5,4,2,3,0,1:T(8,128)} %bitcast.125), calls=%async_computation.1 | async-start | bytes 2097152 | tf_op jit(solution)/shard_map/all_to_all | solution.py:118
  120.2 8.5 %while.34 = (s32[]{:T(128)}, f32[2,2,8,8]{3,1,2,0:T(2,128)S(1)}, f32[2,2,8,8]{3,1,2,0:T(2,128)S(1)}, f32[2,2,8,8,128]{4,3,1,2,0:T(8,128)S(1)}, s32[2]{0:T(128)S(...) while((s32[]{:T(128)}, f32[2,2,8,8]{3,1,2,0:T(2,128)S(1)}, ...), condition=%wide.region_9.10_spmd.clone, body=%wide.region_6.0_spmd.clone.sunk | while | flops 68684800 | bytes 14506174 | solution.py:105
  120.2 2.5 %constant_dynamic-slice_fusion.7 = (bf16[2,512,8,128]{3,2,1,0:T(8,128)(2,1)S(1)}, bf16[2,512,8,128]{3,2,1,0:T(8,128)(2,1)S(1)}) fusion(bf16[2,1024,8,128]{3,2,1,0:T(8,128)(2,1)} %get-tuple-element.537, s32[]{:T(128)S(6)} %select_n.60, bf16[2,1024,8,128]{3,2,1,0:T(8,128)(2,1)} %get-tuple-element.535), kind=kLoop, calls=%fused_computation.41.clone.1 | loop fusion | bytes 8388612 | tf_op jit(solution)/shard_map/while/body/eval_jaxpr/dynamic_slice | solution.py:95
  122.8 0.8 fusion.55
  123.6 0.3 convert_reduce_fusion.6
  123.9 0.6 fusion.57
  124.5 2.5 %constant_dynamic-slice_fusion.7 = (bf16[2,512,8,128]{3,2,1,0:T(8,128)(2,1)S(1)}, bf16[2,512,8,128]{3,2,1,0:T(8,128)(2,1)S(1)}) fusion(bf16[2,1024,8,128]{3,2,1,0:T(8,128)(2,1)} %get-tuple-element.537, s32[]{:T(128)S(6)} %select_n.60, bf16[2,1024,8,128]{3,2,1,0:T(8,128)(2,1)} %get-tuple-element.535), kind=kLoop, calls=%fused_computation.41.clone.1 | loop fusion | bytes 8388612 | tf_op jit(solution)/shard_map/while/body/eval_jaxpr/dynamic_slice | solution.py:95
  127.0 0.8 fusion.55
  127.8 0.3 convert_reduce_fusion.6
  128.1 0.6 fusion.57
  128.8 17.4 %all-to-all-done.1 = f32[1,64,2,2,8,128]{5,4,2,3,0,1:T(8,128)} async-done(((f32[1,64,2,2,8,128]{5,4,2,3,0,1:T(8,128)}), f32[1,64,2,2,8,128]{5,4,2,3,0,1:T(8,128)}, u32[]{:S(2)}, u32[]{:S(2)}) %all-to-all-start.1) | async-done | bytes 1048608 | tf_op jit(solution)/shard_map/all_to_all | solution.py:118
  146.1 2.0 %fusion.27 = f32[8,2,2,8,128]{4,0,3,1,2:T(8,128)S(1)} fusion(f32[8,8,2,2,8,128]{5,4,2,3,1,0:T(8,128)} %bitcast.7, f32[8,8,2,2,8]{1,0,4,2,3:T(8,128)S(1)} %get-tuple-element.371), kind=kLoop, calls=%fused_computation.55 | loop fusion | flops 491520 | bytes 1187840 | tf_op jit(solution)/shard_map/reduce_sum | solution.py:35
  148.1 0.7 copy.137
  148.8 3.3 %all-to-all-start.3 = ((f32[8,2,2,8,128]{4,3,1,2,0:T(8,128)}), f32[8,2,2,8,128]{4,3,1,2,0:T(8,128)S(1)}, u32[]{:S(2)}, u32[]{:S(2)}) async-start(f32[8,2,2,8,128]{4,3,1,2,0:T(8,128)} %copy.137), calls=%async_computation.3 | async-start | bytes 262144 | tf_op jit(solution)/shard_map/all_to_all | solution.py:124
  152.2 4.5 %all-to-all-done.3 = f32[8,2,2,8,128]{4,3,1,2,0:T(8,128)S(1)} async-done(((f32[8,2,2,8,128]{4,3,1,2,0:T(8,128)}), f32[8,2,2,8,128]{4,3,1,2,0:T(8,128)S(1)}, u32[]{:S(2)}, u32[]{:S(2)}) %all-to-all-start.3) | async-done | bytes 131104 | tf_op jit(solution)/shard_map/all_to_all | solution.py:124
  156.7 0.3 fusion.24
  157.1 0.6 reshape.98
  (48 shorter events, 1.4 us)
Async XLA Ops:
  0.0 156.7 %copy-start = (bf16[2,2,8,128]{3,2,1,0:T(8,128)(2,1)S(1)}, bf16[2,2,8,128]{3,2,1,0:T(8,128)(2,1)}, u32[]{:S(2)}) copy-start(bf16[2,2,8,128]{3,2,1,0:T(8,128)(2,1)} %param.18) | copy-start | bytes 24580
  1.5 8.4 %all-to-all-start = ((bf16[2,2,8,1024]{3,1,0,2:T(2,128)(2,1)}), bf16[2,2,8,1024]{3,1,0,2:T(2,128)(2,1)S(1)}, u32[]{:S(2)}, u32[]{:S(2)}) async-start(bf16[2,2,8,1024]{3,1,0,2:T(2,128)(2,1)} %bitcast.126), calls=%async_computation | async-start | bytes 131072 | tf_op jit(solution)/shard_map/all_to_all | solution.py:84
  42.7 50.7 %copy-start.2 = (bf16[2,2,8192]{2,1,0:T(2,128)(2,1)S(1)}, bf16[2,2,8192]{2,1,0:T(2,128)(2,1)}, u32[]{:S(2)}) copy-start(bf16[2,2,8192]{2,1,0:T(2,128)(2,1)} %param.12) | copy-start | bytes 196612
  42.8 62.3 %copy-start.4 = (bf16[2,2,8,128]{3,2,1,0:T(8,128)(2,1)S(1)}, bf16[2,2,8,128]{3,2,1,0:T(8,128)(2,1)}, u32[]{:S(2)}) copy-start(bf16[2,2,8,128]{3,2,1,0:T(8,128)(2,1)} %param.17) | copy-start | bytes 24580
  45.0 1.9 %copy-start.1 = (f32[2,512,64,2,8]{1,2,4,3,0:T(8,128)}, f32[2,512,64,2,8]{1,2,4,3,0:T(8,128)S(1)}, u32[]{:S(2)}) copy-start(f32[2,512,64,2,8]{1,2,4,3,0:T(8,128)S(1)} %get-tuple-element.484) | copy-start | bytes 12582916 | tf_op jit(solution)/shard_map/while
  53.5 1.9 %copy-start.1 = (f32[2,512,64,2,8]{1,2,4,3,0:T(8,128)}, f32[2,512,64,2,8]{1,2,4,3,0:T(8,128)S(1)}, u32[]{:S(2)}) copy-start(f32[2,512,64,2,8]{1,2,4,3,0:T(8,128)S(1)} %get-tuple-element.484) | copy-start | bytes 12582916 | tf_op jit(solution)/shard_map/while
  62.1 1.9 %copy-start.1 = (f32[2,512,64,2,8]{1,2,4,3,0:T(8,128)}, f32[2,512,64,2,8]{1,2,4,3,0:T(8,128)S(1)}, u32[]{:S(2)}) copy-start(f32[2,512,64,2,8]{1,2,4,3,0:T(8,128)S(1)} %get-tuple-element.484) | copy-start | bytes 12582916 | tf_op jit(solution)/shard_map/while
  70.7 1.9 %copy-start.1 = (f32[2,512,64,2,8]{1,2,4,3,0:T(8,128)}, f32[2,512,64,2,8]{1,2,4,3,0:T(8,128)S(1)}, u32[]{:S(2)}) copy-start(f32[2,512,64,2,8]{1,2,4,3,0:T(8,128)S(1)} %get-tuple-element.484) | copy-start | bytes 12582916 | tf_op jit(solution)/shard_map/while
  77.0 43.1 %copy-start.3 = (s32[2]{0:T(128)S(1)}, s32[2]{0:T(128)}, u32[]{:S(2)}) copy-start(s32[2]{0:T(128)} %param.19) | copy-start | bytes 28
  78.0 12.1 %all-to-all-start.2 = ((f32[8,1,256]{2,1,0:T(1,128)}), f32[8,1,256]{2,1,0:T(1,128)S(1)}, u32[]{:S(2)}, u32[]{:S(2)}) async-start(f32[8,1,256]{2,1,0:T(1,128)} %reshape.106), calls=%async_computation.2 | async-start | bytes 16384 | tf_op jit(solution)/shard_map/all_to_all | solution.py:116
  90.1 9.8 %all-to-all-start.5 = ((f32[8,1,256]{2,1,0:T(1,128)}), f32[8,1,256]{2,1,0:T(1,128)S(1)}, u32[]{:S(2)}, u32[]{:S(2)}) async-start(f32[8,1,256]{2,1,0:T(1,128)} %reshape.108), calls=%async_computation.5 | async-start | bytes 16384 | tf_op jit(solution)/shard_map/all_to_all | solution.py:117
  101.8 7.1 %all-to-all-start.6 = ((f32[8,2,2,8]{3,2,1,0:T(2,128)}), f32[8,2,2,8]{3,2,1,0:T(2,128)S(1)}, u32[]{:S(2)}, u32[]{:S(2)}) async-start(f32[8,2,2,8]{3,2,1,0:T(2,128)} %copy.153), calls=%async_computation.6 | async-start | bytes 32768 | tf_op jit(solution)/shard_map/all_to_all | solution.py:123
  108.8 7.1 %all-to-all-start.4 = ((f32[8,2,2,8]{3,2,1,0:T(2,128)}), f32[8,2,2,8]{3,2,1,0:T(2,128)S(1)}, u32[]{:S(2)}, u32[]{:S(2)}) async-start(f32[8,2,2,8]{3,2,1,0:T(2,128)} %copy.140), calls=%async_computation.4 | async-start | bytes 32768 | tf_op jit(solution)/shard_map/all_to_all | solution.py:122
  115.9 30.2 %all-to-all-start.1 = ((f32[1,64,2,2,8,128]{5,4,2,3,0,1:T(8,128)}), f32[1,64,2,2,8,128]{5,4,2,3,0,1:T(8,128)}, u32[]{:S(2)}, u32[]{:S(2)}) async-start(f32[1,64,2,2,8,128]{5,4,2,3,0,1:T(8,128)} %bitcast.125), calls=%async_computation.1 | async-start | bytes 2097152 | tf_op jit(solution)/shard_map/all_to_all | solution.py:118
  148.8 7.9 %all-to-all-start.3 = ((f32[8,2,2,8,128]{4,3,1,2,0:T(8,128)}), f32[8,2,2,8,128]{4,3,1,2,0:T(8,128)S(1)}, u32[]{:S(2)}, u32[]{:S(2)}) async-start(f32[8,2,2,8,128]{4,3,1,2,0:T(8,128)} %copy.137), calls=%async_computation.3 | async-start | bytes 262144 | tf_op jit(solution)/shard_map/all_to_all | solution.py:124
where the time goes:
time: 159 us; the launch traced here: 158 us
  waiting for transfers between devices  40.9 us (26%)
  blocking collectives  32.3 us (20%)
  local copies, waits for them, and re-layouts  28 us (18%)
  starting transfers between devices  27.2 us (17%)
  matrix products  18.9 us (12%)
  other arithmetic  9.79 us (6%)
    all_gather x1, blocking collectives, local(): lax.all_gather(local_rows, 'ctx', axis=0, tiled=True)  32.3 us
    all_to_all x1, waiting for transfers between devices, local(): lax.all_to_all(found[2][None], 'ctx', split_axis=1, concat_axis=0, tiled=...  17.4 us
    dot_general x7, matrix products, block_part(): jnp.einsum(form, weights, values, preferred_element_type=jnp.float32)  13.7 us
    while x8, local copies, waits for them, and re-layouts  7.69 us
    reduce_sum x7, other arithmetic, block_part(): block_total = jnp.sum(weights, axis=-1, dtype=jnp.float32)  5.84 us
    all_to_all x1, starting transfers between devices, local(): lax.all_to_all(found[0][None], 'ctx', split_axis=1, concat_axis=0, tiled=...  5.6 us
    dynamic_slice x4, local copies, waits for them, and re-layouts, prompt_part(): result, _ = lax.scan(prompt_step, initial, (key_blocks, value_blocks))  5.59 us
    all_to_all x1, waiting for transfers between devices, local(): lax.all_to_all(found[0][None], 'ctx', split_axis=1, concat_axis=0, tiled=...  5.54 us
  transfers between devices with their start and end apart: 7, of which 7 were waited for; matrix products, arithmetic and copies ran while one was open for 9% of the time, Pallas kernels for 0%

commit v1 on v0

v1 whole, which is shorter than its diff:
```python
import functools

import jax
import jax.numpy as jnp
from jax import lax
from jax.experimental import pallas as pl
from jax.experimental.pallas import tpu as pltpu
from jax.sharding import PartitionSpec as P

MESH = pl.DeviceIdType.MESH
MASKED_SCORE = -1e30
FLOOR = -1e29
LOG2E = 1.4426950408889634
F32 = jnp.float32
BF16 = jnp.bfloat16
NT = (((1,), (1,)), ((), ()))


def dot_nt(left, right):
    return lax.dot_general(left, right, NT, preferred_element_type=F32)


def dot(left, right):
    return jnp.dot(left, right, preferred_element_type=F32)


def kernel(
    sizes,
    q_ref,
    nk_ref,
    nv_ref,
    len_ref,
    pk_hbm,
    pv_hbm,
    sk_hbm,
    sv_hbm,
    out_ref,
    pk_raw,
    pv_raw,
    sk,
    sv,
    keys,
    values_t,
    place,
    qbuf,
    own_o,
    own_s,
    xo_send,
    xs_send,
    xo_recv,
    xs_recv,
    zo_send,
    zs_send,
    zo_recv,
    zs_recv,
    fo,
    fs,
    po_recv,
    ps_recv,
    stat_rows,
    suf_o,
    suf_m,
    suf_l,
    load_sem,
    g1_send,
    g1_recv,
    g2_send,
    g2_recv,
    gx_send,
    gx_recv,
    xo_sem,
    xs_sem,
    zo_sem,
    zs_sem,
    po_sem,
    ps_sem,
):
    ctx_n, dec_n, groups, rows, head_dim, kv_heads, per_group, steps, own = sizes
    pairs = ctx_n // 2
    unit = dec_n * rows
    positions = keys.shape[1]
    suffix_rows = sk.shape[1]
    scale = head_dim ** (-0.5) * LOG2E
    c = lax.axis_index("ctx")
    d = lax.axis_index("dec")
    z = c // 2
    x = c % 2

    def at_z(j, half):
        other = lax.bitwise_xor(z, jnp.int32(j))
        return other * 2 + (x if half == 0 else 1 - x)

    def dec_of(j):
        return lax.bitwise_xor(d, jnp.int32(j))

    loads = []
    for i, (src, dst) in enumerate(((pk_hbm, pk_raw), (pv_hbm, pv_raw))):
        loads.append(pltpu.make_async_copy(src, dst, load_sem.at[i]))
    for s in range(own):
        for i, (src, dst) in enumerate(((sk_hbm, sk), (sv_hbm, sv))):
            loads.append(pltpu.make_async_copy(src.at[s], dst.at[s], load_sem.at[2 + 2 * s + i]))
    for load in loads:
        load.start()

    barrier = pltpu.get_barrier_semaphore()
    partners = [(c, dec_of(j)) for j in range(1, dec_n)]
    partners += [(at_z(j, 0), d) for j in range(1, pairs)]
    partners += [(at_z(0, 1), d)]
    for partner in partners:
        pl.semaphore_signal(barrier, inc=1, device_id=partner, device_id_type=MESH)
    pl.semaphore_wait(barrier, len(partners))

    def remote(src, dst, send_sem, recv_sem, target):
        return pltpu.make_async_remote_copy(
            src_ref=src, dst_ref=dst, send_sem=send_sem, recv_sem=recv_sem,
            device_id=target, device_id_type=MESH,
        )

    own_rows = pl.ds(pl.multiple_of(d * rows, rows), rows)
    g1 = []
    for j in range(1, dec_n):
        copy = remote(q_ref.at[dec_of(j)], qbuf.at[c, :, own_rows, :],
                      g1_send.at[j], g1_recv.at[j], (c, dec_of(j)))
        copy.start()
        g1.append(copy)
    qbuf[c, :, own_rows, :] = q_ref[d]
    for copy in g1:
        copy.wait()
    g2 = {}
    for j in range(1, pairs):
        g2[j] = remote(qbuf.at[c], qbuf.at[c], g2_send.at[j], g2_recv.at[j], (at_z(j, 0), d))
        g2[j].start()
    gx = {}

    def forward(j):
        if j:
            g2[j].wait_recv()
        here = at_z(j, 0)
        gx[j] = remote(qbuf.at[here], qbuf.at[here], gx_send.at[j], gx_recv.at[j], (at_z(0, 1), d))
        gx[j].start()

    forward(0)

    span = 256 // groups
    perm_r = lax.broadcasted_iota(jnp.int32, (256, 256), 0)
    perm_i = lax.broadcasted_iota(jnp.int32, (256, 256), 1)
    perm = ((perm_r % span) * groups + perm_r // span == perm_i).astype(BF16)
    eye = (lax.broadcasted_iota(jnp.int32, (head_dim, head_dim), 0)
           == lax.broadcasted_iota(jnp.int32, (head_dim, head_dim), 1)).astype(BF16)
    loads[0].wait()
    loads[1].wait()

    def prepare(b, carry):
        raw = pl.ds(pl.multiple_of(b * 256, 256), 256)
        there = pl.ds(pl.multiple_of(b * span, span), span)
        key_rows = dot(perm, pk_raw[raw, :]).astype(BF16)
        value_rows = dot(perm, pv_raw[raw, :]).astype(BF16)
        turned = dot_nt(eye, value_rows).astype(BF16)
        for g in range(groups):
            keys[g, there, :] = key_rows[g * span:(g + 1) * span]
            values_t[g, :head_dim, there] = turned[:, g * span:(g + 1) * span]
        return carry

    lax.fori_loop(0, positions * groups // 256, prepare, 0)
    values_t[:, head_dim:, :] = jnp.ones_like(values_t[:, head_dim:, :])

    forward(1)

    chunk = min(512, suffix_rows // kv_heads) * kv_heads
    per_row = steps * per_group
    q_rows = kv_heads * per_row
    line = lax.broadcasted_iota(jnp.int32, (q_rows, chunk), 0) // per_row
    column = lax.broadcasted_iota(jnp.int32, (q_rows, chunk), 1)
    place[...] = jnp.where(column % kv_heads == line, column // kv_heads, 1 << 30)
    ones = jnp.ones((chunk, head_dim), BF16)

    def suffix(s):
        loads[2 + 2 * s].wait()
        loads[3 + 2 * s].wait()
        q = q_ref[:, :, s * per_row:(s + 1) * per_row, :].reshape(q_rows, head_dim)
        length = len_ref[s]

        def part(scores, visible, values, many):
            masked = jnp.where(visible, scores, MASKED_SCORE)
            top = jnp.maximum(jnp.max(masked, axis=1, keepdims=True), FLOOR)
            weights = jnp.exp2((masked - top) * scale).astype(BF16)
            return top, dot(weights, many), dot(weights, values)

        def merge(left, right):
            top = jnp.maximum(left[0], right[0])
            a = jnp.exp2((left[0] - top) * scale)
            b = jnp.exp2((right[0] - top) * scale)
            return top, left[1] * a + right[1] * b, left[2] * a + right[2] * b

        new_rows = steps * kv_heads
        col = lax.broadcasted_iota(jnp.int32, (q_rows, new_rows), 1)
        row = lax.broadcasted_iota(jnp.int32, (q_rows, new_rows), 0)
        seen = (col % kv_heads == row // per_row) & (col // kv_heads <= (row % per_row) // per_group)
        state = part(dot_nt(q, nk_ref[s]), seen, nv_ref[s], jnp.ones((new_rows, head_dim), BF16))
        for b in range(suffix_rows // chunk):
            here = slice(b * chunk, (b + 1) * chunk)
            visible = place[...] < length - b * (chunk // kv_heads)
            state = merge(state, part(dot_nt(q, sk[s, here, :]), visible, sv[s, here, :], ones))
        mine = slice(s * per_row, (s + 1) * per_row)
        shape = (kv_heads, per_row, head_dim)
        suf_o[:, mine, :] = state[2].reshape(shape)
        suf_l[:, mine, :] = state[1].reshape(shape)
        suf_m[:, mine, :] = jnp.broadcast_to(state[0] * scale, (q_rows, head_dim)).reshape(shape)

    suffix(0)
    for j in range(2, pairs):
        forward(j)
    for s in range(1, own):
        suffix(s)

    block = min(512, positions)

    def tile(j):
        mine, theirs = at_z(j, 0), at_z(j, 1)

        def group(g, carry):
            q = jnp.concatenate([qbuf[mine, g], qbuf[theirs, g]], axis=0)
            tops, sums = [], []
            for b in range(positions // block):
                here = slice(b * block, (b + 1) * block)
                scores = dot_nt(keys[g, here, :], q)
                top = jnp.max(scores, axis=0, keepdims=True)
                weights = jnp.exp2((scores - top) * scale).astype(BF16)
                tops.append(top * scale)
                sums.append(dot(values_t[g, :, here], weights))
            top = functools.reduce(jnp.maximum, tops)
            total = sum(one * jnp.exp2(m - top) for one, m in zip(sums, tops))
            stats = jnp.concatenate([
                jnp.broadcast_to(top, (4, 2 * unit)), total[head_dim:head_dim + 4]], axis=0)
            total = total[:head_dim]
            own_o[j, g] = total[:, :unit]
            own_s[j, g] = stats[:, :unit]
            xo_send[j, g] = total[:, unit:].astype(BF16)
            xs_send[j, g] = stats[:, unit:]
            return carry

        lax.fori_loop(0, groups, group, 0)

    xs = {}
    zs = {}

    def send_x(j):
        target = (at_z(0, 1), d)
        xs[j] = (
            remote(xo_send.at[j], xo_recv.at[j], xo_sem.at[0, j], xo_sem.at[1, j], target),
            remote(xs_send.at[j], xs_recv.at[j], xs_sem.at[0, j], xs_sem.at[1, j], target),
        )
        for copy in xs[j]:
            copy.start()

    def merged(parts):
        top = functools.reduce(jnp.maximum, [stats[0:1] for _, stats in parts])
        total, weight = 0.0, 0.0
        for sums, stats in parts:
            factor = jnp.exp2(stats[0:1] - top)
            total = total + sums.astype(F32) * factor
            weight = weight + stats[4:5] * factor
        width = top.shape[1]
        return total, jnp.concatenate(
            [jnp.broadcast_to(top, (4, width)), jnp.broadcast_to(weight, (4, width))], axis=0)

    def merge_x(j):
        for copy in xs[j]:
            copy.wait_recv()
        for g in range(groups):
            total, stats = merged([(own_o[j, g], own_s[j, g]), (xo_recv[j, g], xs_recv[j, g])])
            if j:
                zo_send[j, g] = total.astype(BF16)
                zs_send[j, g] = stats
            else:
                own_o[j, g] = total
                own_s[j, g] = stats
        if j:
            target = (at_z(j, 0), d)
            zs[j] = (
                remote(zo_send.at[j], zo_recv.at[j], zo_sem.at[0, j], zo_sem.at[1, j], target),
                remote(zs_send.at[j], zs_recv.at[j], zs_sem.at[0, j], zs_sem.at[1, j], target),
            )
            for copy in zs[j]:
                copy.start()

    order = list(range(1, pairs)) + [0]
    for i, j in enumerate(order):
        gx[j].wait_recv()
        tile(j)
        send_x(j)
        if i:
            merge_x(order[i - 1])
    merge_x(0)

    for j in range(1, pairs):
        for copy in zs[j]:
            copy.wait_recv()
    for g in range(groups):
        total, stats = merged([(own_o[0, g], own_s[0, g])]
                              + [(zo_recv[j, g], zs_recv[j, g]) for j in range(1, pairs)])
        fo[g] = total.T
        fs[g] = stats
    ps = []
    for j in range(1, dec_n):
        target = dec_of(j)
        there = pl.ds(pl.multiple_of(target * rows, rows), rows)
        ps.append(remote(fo.at[:, there, :], po_recv.at[d], po_sem.at[0, j], po_sem.at[1, j],
                         (c, target)))
        ps.append(remote(fs, ps_recv.at[d], ps_sem.at[0, j], ps_sem.at[1, j], (c, target)))
    for copy in ps:
        copy.start()
    po_recv[d] = fo[:, own_rows, :]
    ps_recv[d] = fs[...]
    for copy in ps:
        copy.wait_recv()
    flat = ps_recv[...].reshape(kv_heads * 8, unit)
    stat_rows[...] = flat.T
    picked = stat_rows[own_rows, :]
    for a in range(dec_n):
        for g in range(groups):
            h = a * groups + g
            top_p = picked[:, h * 8:h * 8 + 1]
            sum_p = picked[:, h * 8 + 4:h * 8 + 5]
            top = jnp.maximum(top_p, suf_m[h])
            left = jnp.exp2(top_p - top)
            right = jnp.exp2(suf_m[h] - top)
            result = (po_recv[a, g] * left + suf_o[h] * right) / (sum_p * left + suf_l[h] * right)
            out_ref[a, g] = result.astype(BF16)

    for copy in list(g2.values()) + list(gx.values()):
        copy.wait_send()
    for both in list(xs.values()) + list(zs.values()):
        for copy in both:
            copy.wait_send()
    for copy in ps:
        copy.wait_send()


def local(ctx_n, dec_n, queries, prompt_keys, prompt_values, suffix_keys, suffix_values,
          new_keys, new_values, lengths):
    own, steps, features = queries.shape
    positions, groups, head_dim = prompt_keys.shape
    suffix_length, kv_heads = suffix_keys.shape[1:3]
    per_group = features // (kv_heads * head_dim)
    rows = own * steps * per_group
    unit = dec_n * rows
    pairs = ctx_n // 2
    sent = (
        queries.reshape(own, steps, dec_n, groups, per_group, head_dim)
        .transpose(2, 3, 0, 1, 4, 5)
        .reshape(dec_n, groups, rows, head_dim)
    )
    suffix_rows = suffix_length * kv_heads
    q_rows = kv_heads * steps * per_group
    chunk = min(512, suffix_length) * kv_heads
    sizes = (ctx_n, dec_n, groups, rows, head_dim, kv_heads, per_group, steps, own)
    vmem = pl.BlockSpec(memory_space=pltpu.VMEM)
    anywhere = pl.BlockSpec(memory_space=pl.ANY)
    dma = pltpu.SemaphoreType.DMA
    moved = (pairs, groups, head_dim, unit)
    noted = (pairs, groups, 8, unit)
    result = pl.pallas_call(
        functools.partial(kernel, sizes),
        out_shape=jax.ShapeDtypeStruct((dec_n, groups, rows, head_dim), BF16),
        in_specs=[vmem, vmem, vmem, pl.BlockSpec(memory_space=pltpu.SMEM)] + [anywhere] * 4,
        out_specs=vmem,
        scratch_shapes=[
            pltpu.VMEM((positions * groups, head_dim), BF16),
            pltpu.VMEM((positions * groups, head_dim), BF16),
            pltpu.VMEM((own, suffix_rows, head_dim), BF16),
            pltpu.VMEM((own, suffix_rows, head_dim), BF16),
            pltpu.VMEM((groups, positions, head_dim), BF16),
            pltpu.VMEM((groups, head_dim + 16, positions), BF16),
            pltpu.VMEM((q_rows, chunk), jnp.int32),
            pltpu.VMEM((ctx_n, groups, unit, head_dim), BF16),
            pltpu.VMEM(moved, F32),
            pltpu.VMEM(noted, F32),
            pltpu.VMEM(moved, BF16),
            pltpu.VMEM(noted, F32),
            pltpu.VMEM(moved, BF16),
            pltpu.VMEM(noted, F32),
            pltpu.VMEM(moved, BF16),
            pltpu.VMEM(noted, F32),
            pltpu.VMEM(moved, BF16),
            pltpu.VMEM(noted, F32),
            pltpu.VMEM((groups, unit, head_dim), F32),
            pltpu.VMEM((groups, 8, unit), F32),
            pltpu.VMEM((dec_n, groups, rows, head_dim), F32),
            pltpu.VMEM((dec_n, groups, 8, unit), F32),
            pltpu.VMEM((unit, kv_heads * 8), F32),
            pltpu.VMEM((kv_heads, rows, head_dim), F32),
            pltpu.VMEM((kv_heads, rows, head_dim), F32),
            pltpu.VMEM((kv_heads, rows, head_dim), F32),
            dma((2 + 2 * own,)),
            dma((dec_n,)),
            dma((dec_n,)),
            dma((pairs,)),
            dma((pairs,)),
            dma((pairs,)),
            dma((pairs,)),
            dma((2, pairs)),
            dma((2, pairs)),
            dma((2, pairs)),
            dma((2, pairs)),
            dma((2, dec_n)),
            dma((2, dec_n)),
        ],
        compiler_params=pltpu.CompilerParams(
            collective_id=0, has_side_effects=True, vmem_limit_bytes=56 * 1024 * 1024
        ),
    )(
        sent,
        new_keys.reshape(own, steps * kv_heads, head_dim),
        new_values.reshape(own, steps * kv_heads, head_dim),
        lengths,
        prompt_keys.reshape(positions * groups, head_dim),
        prompt_values.reshape(positions * groups, head_dim),
        suffix_keys.reshape(own, suffix_rows, head_dim),
        suffix_values.reshape(own, suffix_rows, head_dim),
    )
    return (
        result.reshape(dec_n, groups, own, steps, per_group, head_dim)
        .transpose(2, 3, 0, 1, 4, 5)
        .reshape(own, steps, features)
    )


def solution(mesh):
    return jax.shard_map(
        functools.partial(local, mesh.shape["ctx"], mesh.shape["dec"]),
        mesh=mesh,
        in_specs=(
            P(("ctx", "dec"), None, None),
            P("ctx", "dec", None),
            P("ctx", "dec", None),
            P(("ctx", "dec"), None, None, None),
            P(("ctx", "dec"), None, None, None),
            P(("ctx", "dec"), None, None, None),
            P(("ctx", "dec"), None, None, None),
            P(("ctx", "dec")),
        ),
        out_specs=P(("ctx", "dec"), None, None),
        check_vma=False,
    )
```

time: 159 us -> 47.9 us (0.30)
  Pallas kernels: 0 us -> 44.6 us
  waiting for transfers between devices: 40.9 us -> 0 us
  blocking collectives: 32.3 us -> 0 us
  starting transfers between devices: 27.2 us -> 0 us
  local copies, waits for them, and re-layouts: 28 us -> 3.04 us
  matrix products: 18.9 us -> 0 us
  other arithmetic: 9.79 us -> 0 us
    pallas_call x0 -> x1, Pallas kernels: none -> 44.6 us  [local(): pl.pallas_call(functools.partial(kernel, sizes), out_shape=jax.ShapeDtype...]
    all_to_all x7 -> x0, waiting for transfers between devices: 40.9 us -> none  [the longest x1 17.4 us: local(): lax.all_to_all(found[2][None], 'ctx', split_axis=1, concat_axis=0, tiled=...]
    all_gather x1 -> x0, blocking collectives: 32.3 us -> none  [local(): lax.all_gather(local_rows, 'ctx', axis=0, tiled=True)]
    all_to_all x7 -> x0, starting transfers between devices: 27.2 us -> none  [the longest x1 5.6 us: local(): lax.all_to_all(found[0][None], 'ctx', split_axis=1, concat_axis=0, tiled=...]
    dot_general x14 -> x0, matrix products: 18.9 us -> none  [the longest x7 13.7 us: block_part(): jnp.einsum(form, weights, values, preferred_element_type=jnp.float32)]
    dynamic_slice x6 -> x0, local copies, waits for them, and re-layouts: 10.6 us -> none  [the longest x4 5.59 us: prompt_part(): result, _ = lax.scan(prompt_step, initial, (key_blocks, value_blocks))]
    while x11 -> x0, local copies, waits for them, and re-layouts: 9.56 us -> none
    reduce_sum x9 -> x0, other arithmetic: 7.89 us -> none  [the longest x7 5.84 us: block_part(): block_total = jnp.sum(weights, axis=-1, dtype=jnp.float32)]
  transfers between devices with their start and end apart: 7 -> 0, of which waited for: 7 -> 0; matrix products, arithmetic and copies ran while one was open for 9% -> 0% of each run, Pallas kernels for 0% -> 0%
where the time goes in v1:
time: 47.9 us; the launch traced here: 47.7 us
  Pallas kernels  44.6 us (93%)
  local copies, waits for them, and re-layouts  3.04 us (6%)
    pallas_call x1, Pallas kernels, local(): pl.pallas_call(functools.partial(kernel, sizes), out_shape=jax.ShapeDtype...  44.6 us
    reshape x2, local copies, waits for them, and re-layouts, local(): queries.reshape(own, steps, dec_n, groups, per_group, head_dim)  1.54 us

profile of v1, /device:TPU:0, one launch (start us, length us, event | category | flops | bytes accessed | tf_op | source)
XLA Modules:
  0.0 47.7 jit_solution(4591579154886891116)
XLA Ops:
  0.0 0.9 %reshape.30 = bf16[2,2,4,2,8,128]{5,4,3,2,1,0:T(8,128)(2,1)S(1)} reshape(bf16[2,2,8192]{2,1,0:T(2,128)(2,1)} %param.8) | data formatting | bytes 131072 | tf_op jit(solution)/shard_map/reshape | solution.py:350
  0.9 0.6 %copy.9 = bf16[2,2,4,2,8,128]{5,4,1,0,3,2:T(8,128)(2,1)} copy(bf16[2,2,4,2,8,128]{5,4,3,2,1,0:T(8,128)(2,1)S(1)} %reshape.30) | data formatting | bytes 131072 | tf_op jit(solution)/shard_map/reshape | solution.py:350
  1.5 44.6 %shard_map.82 = bf16[4,2,32,128]{3,2,1,0:T(8,128)(2,1)} custom-call(bf16[4,2,32,128]{3,2,1,0:T(8,128)(2,1)} %bitcast.18, bf16[2,16,128]{2,1,0:T(8,128)(2,1)} %bitcast.20, bf16[2,16,128]{2,1,0:T(8,128)(2,1)} %bitcast.21, s32[2]{0:T(128)} %len_ref.1, bf16[4096,128]{1,0:T(8,128)(2,1)} %bitcast.16, bf16[4096,128]{1,0:T(8,128)(2,1)} %bitcast.17, ...), custom_call_target="tpu_custom_call" | custom-call | tf_op jit(solution)/shard_map/pallas_call | solution.py:363
  46.2 0.9 %copy.10 = bf16[2,2,4,2,8,128]{5,4,3,2,1,0:T(8,128)(2,1)S(1)} copy(bf16[2,2,4,2,8,128]{5,4,1,0,3,2:T(8,128)(2,1)} %bitcast.19) | data formatting | bytes 131072 | tf_op jit(solution)/shard_map/transpose | solution.py:424
  47.0 0.6 %reshape.39 = bf16[2,2,8192]{2,1,0:T(2,128)(2,1)} reshape(bf16[2,2,4,2,8,128]{5,4,3,2,1,0:T(8,128)(2,1)S(1)} %copy.10) | data formatting | bytes 131072 | tf_op jit(solution)/shard_map/reshape | solution.py:425

commit v2 on v1

--- a/solution.py
+++ b/solution.py
@@ -41,7 +41,6 @@
     sv,
     keys,
     values_t,
-    place,
     qbuf,
     own_o,
     own_s,
@@ -116,14 +115,47 @@
             device_id=target, device_id_type=MESH,
         )
 
+    span = 256 // groups
+    perm_r = lax.broadcasted_iota(jnp.int32, (256, 256), 0)
+    perm_i = lax.broadcasted_iota(jnp.int32, (256, 256), 1)
+    perm = ((perm_r % span) * groups + perm_r // span == perm_i).astype(BF16)
+    eye = (lax.broadcasted_iota(jnp.int32, (head_dim, head_dim), 0)
+           == lax.broadcasted_iota(jnp.int32, (head_dim, head_dim), 1)).astype(BF16)
+
+    def prepare_keys(raw, there):
+        key_rows = dot(perm, pk_raw[raw, :]).astype(BF16)
+        for g in range(groups):
+            keys[g, there, :] = key_rows[g * span:(g + 1) * span]
+
+    def prepare_values(raw, there):
+        value_rows = dot(perm, pv_raw[raw, :]).astype(BF16)
+        turned = dot_nt(eye, value_rows).astype(BF16)
+        for g in range(groups):
+            values_t[g, :head_dim, there] = turned[:, g * span:(g + 1) * span]
+
+    def prepare_all(prepare):
+        count = positions * groups // 256
+        at_once = 8
+
+        def step(i, carry):
+            for k in range(at_once):
+                b = i * at_once + k
+                prepare(pl.ds(pl.multiple_of(b * 256, 256), 256),
+                        pl.ds(pl.multiple_of(b * span, span), span))
+            return carry
+
+        lax.fori_loop(0, count // at_once, step, 0)
+
     own_rows = pl.ds(pl.multiple_of(d * rows, rows), rows)
     g1 = []
     for j in range(1, dec_n):
-        copy = remote(q_ref.at[dec_of(j)], qbuf.at[c, :, own_rows, :],
+        copy = remote(q_ref.at[:, :, dec_of(j)], qbuf.at[c, d],
                       g1_send.at[j], g1_recv.at[j], (c, dec_of(j)))
         copy.start()
         g1.append(copy)
-    qbuf[c, :, own_rows, :] = q_ref[d]
+    qbuf[c, d] = q_ref[:, :, d]
+    loads[0].wait()
+    prepare_all(prepare_keys)
     for copy in g1:
         copy.wait()
     g2 = {}
@@ -141,50 +173,35 @@
 
     forward(0)
 
-    span = 256 // groups
-    perm_r = lax.broadcasted_iota(jnp.int32, (256, 256), 0)
-    perm_i = lax.broadcasted_iota(jnp.int32, (256, 256), 1)
-    perm = ((perm_r % span) * groups + perm_r // span == perm_i).astype(BF16)
-    eye = (lax.broadcasted_iota(jnp.int32, (head_dim, head_dim), 0)
-           == lax.broadcasted_iota(jnp.int32, (head_dim, head_dim), 1)).astype(BF16)
-    loads[0].wait()
     loads[1].wait()
-
-    def prepare(b, carry):
-        raw = pl.ds(pl.multiple_of(b * 256, 256), 256)
-        there = pl.ds(pl.multiple_of(b * span, span), span)
-        key_rows = dot(perm, pk_raw[raw, :]).astype(BF16)
-        value_rows = dot(perm, pv_raw[raw, :]).astype(BF16)
-        turned = dot_nt(eye, value_rows).astype(BF16)
-        for g in range(groups):
-            keys[g, there, :] = key_rows[g * span:(g + 1) * span]
-            values_t[g, :head_dim, there] = turned[:, g * span:(g + 1) * span]
-        return carry
-
-    lax.fori_loop(0, positions * groups // 256, prepare, 0)
+    prepare_all(prepare_values)
     values_t[:, head_dim:, :] = jnp.ones_like(values_t[:, head_dim:, :])
 
     forward(1)
 
     chunk = min(512, suffix_rows // kv_heads) * kv_heads
+    per_step = kv_heads * per_group
+    q_rows = steps * per_step
     per_row = steps * per_group
-    q_rows = kv_heads * per_row
-    line = lax.broadcasted_iota(jnp.int32, (q_rows, chunk), 0) // per_row
-    column = lax.broadcasted_iota(jnp.int32, (q_rows, chunk), 1)
-    place[...] = jnp.where(column % kv_heads == line, column // kv_heads, 1 << 30)
-    ones = jnp.ones((chunk, head_dim), BF16)
+    lane_head = lax.broadcasted_iota(jnp.int32, (per_group, head_dim), 1) % kv_heads
+    hits = [lane_head == g for g in range(kv_heads)]
+    lane_place = lax.broadcasted_iota(jnp.int32, (per_row, head_dim), 1) // kv_heads
+
+    def around(op, folded):
+        shift = kv_heads
+        while shift < head_dim:
+            folded = op(folded, pltpu.roll(folded, shift, 1))
+            shift *= 2
+        return folded
+
+    def by_row(folded):
+        return jnp.concatenate(
+            [folded[t * per_group:(t + 1) * per_group, g:g + 1]
+             for t in range(steps) for g in range(kv_heads)], axis=0)
 
     def suffix(s):
-        loads[2 + 2 * s].wait()
-        loads[3 + 2 * s].wait()
-        q = q_ref[:, :, s * per_row:(s + 1) * per_row, :].reshape(q_rows, head_dim)
+        q = q_ref[s].astype(F32).reshape(q_rows, head_dim).astype(BF16)
         length = len_ref[s]
-
-        def part(scores, visible, values, many):
-            masked = jnp.where(visible, scores, MASKED_SCORE)
-            top = jnp.maximum(jnp.max(masked, axis=1, keepdims=True), FLOOR)
-            weights = jnp.exp2((masked - top) * scale).astype(BF16)
-            return top, dot(weights, many), dot(weights, values)
 
         def merge(left, right):
             top = jnp.maximum(left[0], right[0])
@@ -195,17 +212,53 @@
         new_rows = steps * kv_heads
         col = lax.broadcasted_iota(jnp.int32, (q_rows, new_rows), 1)
         row = lax.broadcasted_iota(jnp.int32, (q_rows, new_rows), 0)
-        seen = (col % kv_heads == row // per_row) & (col // kv_heads <= (row % per_row) // per_group)
-        state = part(dot_nt(q, nk_ref[s]), seen, nv_ref[s], jnp.ones((new_rows, head_dim), BF16))
-        for b in range(suffix_rows // chunk):
-            here = slice(b * chunk, (b + 1) * chunk)
-            visible = place[...] < length - b * (chunk // kv_heads)
-            state = merge(state, part(dot_nt(q, sk[s, here, :]), visible, sv[s, here, :], ones))
-        mine = slice(s * per_row, (s + 1) * per_row)
-        shape = (kv_heads, per_row, head_dim)
-        suf_o[:, mine, :] = state[2].reshape(shape)
-        suf_l[:, mine, :] = state[1].reshape(shape)
-        suf_m[:, mine, :] = jnp.broadcast_to(state[0] * scale, (q_rows, head_dim)).reshape(shape)
+        seen = (col % kv_heads == row // per_group % kv_heads) & (col // kv_heads <= row // per_step)
+        masked = jnp.where(seen, dot_nt(q, nk_ref[s]), MASKED_SCORE)
+        top = jnp.max(masked, axis=1, keepdims=True)
+        weights = jnp.exp2((masked - top) * scale).astype(BF16)
+        state = (top, jnp.sum(weights.astype(F32), axis=1, keepdims=True), dot(weights, nv_ref[s]))
+        loads[2 + 2 * s].wait()
+        loads[3 + 2 * s].wait()
+
+        def part(b, state):
+            here = pl.ds(pl.multiple_of(b * chunk, chunk), chunk)
+            scores = dot_nt(q, sk[s, here, :])
+            left = length - b * (chunk // kv_heads)
+            found = []
+            for k in range(chunk // head_dim):
+                lanes = slice(k * head_dim, (k + 1) * head_dim)
+                picked = []
+                for t in range(steps):
+                    base = t * per_step
+                    one = scores[base:base + per_group, lanes]
+                    for g in range(1, kv_heads):
+                        first = base + g * per_group
+                        one = jnp.where(hits[g], scores[first:first + per_group, lanes], one)
+                    picked.append(one)
+                visible = lane_place < left - k * (head_dim // kv_heads)
+                found.append(jnp.where(visible, jnp.concatenate(picked, axis=0), MASKED_SCORE))
+            top = jnp.maximum(around(jnp.maximum, functools.reduce(jnp.maximum, found)), FLOOR)
+            total = 0.0
+            spread = []
+            for one in found:
+                weights = jnp.exp2((one - top) * scale).astype(BF16).astype(F32)
+                total = total + weights
+                spread.append(jnp.concatenate(
+                    [jnp.where(hits[g], weights[t * per_group:(t + 1) * per_group], 0.0)
+                     for t in range(steps) for g in range(kv_heads)], axis=0).astype(BF16))
+            summed = dot(jnp.concatenate(spread, axis=1), sv[s, here, :])
+            return merge(state, (by_row(top), by_row(around(jnp.add, total)), summed))
+
+        state = lax.fori_loop(0, suffix_rows // chunk, part, state)
+        for t in range(steps):
+            for g in range(kv_heads):
+                first = t * per_step + g * per_group
+                rows_here = slice(first, first + per_group)
+                mine = slice(s * per_row + t * per_group, s * per_row + (t + 1) * per_group)
+                shape = (per_group, head_dim)
+                suf_o[g, mine, :] = state[2][rows_here]
+                suf_l[g, mine, :] = jnp.broadcast_to(state[1][rows_here], shape)
+                suf_m[g, mine, :] = jnp.broadcast_to(state[0][rows_here] * scale, shape)
 
     suffix(0)
     for j in range(2, pairs):
@@ -218,8 +271,10 @@
     def tile(j):
         mine, theirs = at_z(j, 0), at_z(j, 1)
 
-        def group(g, carry):
-            q = jnp.concatenate([qbuf[mine, g], qbuf[theirs, g]], axis=0)
+        for g in range(groups):
+            q = jnp.concatenate(
+                [qbuf[at, :, :, :, g].astype(F32).reshape(unit, head_dim) for at in (mine, theirs)],
+                axis=0).astype(BF16)
             tops, sums = [], []
             for b in range(positions // block):
                 here = slice(b * block, (b + 1) * block)
@@ -237,9 +292,6 @@
             own_s[j, g] = stats[:, :unit]
             xo_send[j, g] = total[:, unit:].astype(BF16)
             xs_send[j, g] = stats[:, unit:]
-            return carry
-
-        lax.fori_loop(0, groups, group, 0)
 
     xs = {}
     zs = {}
@@ -326,7 +378,10 @@
             left = jnp.exp2(top_p - top)
             right = jnp.exp2(suf_m[h] - top)
             result = (po_recv[a, g] * left + suf_o[h] * right) / (sum_p * left + suf_l[h] * right)
-            out_ref[a, g] = result.astype(BF16)
+            for s in range(own):
+                for t in range(steps):
+                    first = (s * steps + t) * per_group
+                    out_ref[s, t, a, g] = result[first:first + per_group].astype(BF16)
 
     for copy in list(g2.values()) + list(gx.values()):
         copy.wait_send()
@@ -346,14 +401,8 @@
     rows = own * steps * per_group
     unit = dec_n * rows
     pairs = ctx_n // 2
-    sent = (
-        queries.reshape(own, steps, dec_n, groups, per_group, head_dim)
-        .transpose(2, 3, 0, 1, 4, 5)
-        .reshape(dec_n, groups, rows, head_dim)
-    )
+    by_head = (own, steps, dec_n, groups, per_group, head_dim)
     suffix_rows = suffix_length * kv_heads
-    q_rows = kv_heads * steps * per_group
-    chunk = min(512, suffix_length) * kv_heads
     sizes = (ctx_n, dec_n, groups, rows, head_dim, kv_heads, per_group, steps, own)
     vmem = pl.BlockSpec(memory_space=pltpu.VMEM)
     anywhere = pl.BlockSpec(memory_space=pl.ANY)
@@ -362,7 +411,7 @@
     noted = (pairs, groups, 8, unit)
     result = pl.pallas_call(
         functools.partial(kernel, sizes),
-        out_shape=jax.ShapeDtypeStruct((dec_n, groups, rows, head_dim), BF16),
+        out_shape=jax.ShapeDtypeStruct(by_head, BF16),
         in_specs=[vmem, vmem, vmem, pl.BlockSpec(memory_space=pltpu.SMEM)] + [anywhere] * 4,
         out_specs=vmem,
         scratch_shapes=[
@@ -372,8 +421,7 @@
             pltpu.VMEM((own, suffix_rows, head_dim), BF16),
             pltpu.VMEM((groups, positions, head_dim), BF16),
             pltpu.VMEM((groups, head_dim + 16, positions), BF16),
-            pltpu.VMEM((q_rows, chunk), jnp.int32),
-            pltpu.VMEM((ctx_n, groups, unit, head_dim), BF16),
+            pltpu.VMEM((ctx_n, dec_n, own, steps, groups, per_group, head_dim), BF16),
             pltpu.VMEM(moved, F32),
             pltpu.VMEM(noted, F32),
             pltpu.VMEM(moved, BF16),
@@ -410,7 +458,7 @@
             collective_id=0, has_side_effects=True, vmem_limit_bytes=56 * 1024 * 1024
         ),
     )(
-        sent,
+        queries.reshape(by_head),
         new_keys.reshape(own, steps * kv_heads, head_dim),
         new_values.reshape(own, steps * kv_heads, head_dim),
         lengths,
@@ -419,11 +467,7 @@
         suffix_keys.reshape(own, suffix_rows, head_dim),
         suffix_values.reshape(own, suffix_rows, head_dim),
     )
-    return (
-        result.reshape(dec_n, groups, own, steps, per_group, head_dim)
-        .transpose(2, 3, 0, 1, 4, 5)
-        .reshape(own, steps, features)
-    )
+    return result.reshape(own, steps, features)
 
 
 def solution(mesh):

time: 47.9 us -> 45.2 us (0.944)
  Pallas kernels: 44.6 us -> 41.9 us
    pallas_call x1, Pallas kernels: 44.6 us -> 41.9 us  [local(): pl.pallas_call(functools.partial(kernel, sizes), out_shape=jax.ShapeDtype...]
    transpose x1 -> x0, local copies, waits for them, and re-layouts: 0.85 us -> none  [local(): return result.reshape(dec_n, groups, own, steps, per_group, head_dim).tra...]
    reshape x3 -> x2, local copies, waits for them, and re-layouts: 2.19 us -> 3.01 us  [the longest x1 1.53 us: local(): queries.reshape(by_head)]
where the time goes in v2:
time: 45.2 us; the launch traced here: 45 us
  Pallas kernels  41.9 us (93%)
  local copies, waits for them, and re-layouts  3.01 us (7%)
    pallas_call x1, Pallas kernels, local(): pl.pallas_call(functools.partial(kernel, sizes), out_shape=jax.ShapeDtype...  41.9 us
    reshape x1, local copies, waits for them, and re-layouts, local(): queries.reshape(by_head)  1.53 us
    reshape x1, local copies, waits for them, and re-layouts, local(): return result.reshape(own, steps, features)  1.49 us

profile of v2, /device:TPU:0, one launch (start us, length us, event | category | flops | bytes accessed | tf_op | source)
XLA Modules:
  0.0 45.0 jit_solution(16300911398380662200)
XLA Ops:
  0.0 1.5 %reshape.24.q_ref = bf16[2,2,4,2,8,128]{5,4,3,2,1,0:T(8,128)(2,1)} reshape(bf16[2,2,8192]{2,1,0:T(2,128)(2,1)} %param.8) | data formatting | bytes 131072 | tf_op jit(solution)/shard_map/reshape | solution.py:461
  1.5 41.9 %shard_map.82 = bf16[2,2,4,2,8,128]{5,4,3,2,1,0:T(8,128)(2,1)} custom-call(bf16[2,2,4,2,8,128]{5,4,3,2,1,0:T(8,128)(2,1)} %reshape.24.q_ref, bf16[2,16,128]{2,1,0:T(8,128)(2,1)} %bitcast.12, bf16[2,16,128]{2,1,0:T(8,128)(2,1)} %bitcast.13, s32[2]{0:T(128)} %len_ref.1, bf16[4096,128]{1,0:T(8,128)(2,1)} %bitcast.10, bf16[4096,128]{1,0:T(8,128)(2,1)} %bitcast.11, ...), custom_call_target="tpu_custom_call" | custom-call | tf_op jit(solution)/shard_map/pallas_call | solution.py:412
  43.5 1.5 %reshape.31 = bf16[2,2,8192]{2,1,0:T(2,128)(2,1)} reshape(bf16[2,2,4,2,8,128]{5,4,3,2,1,0:T(8,128)(2,1)} %shard_map.82) | data formatting | bytes 131072 | tf_op jit(solution)/shard_map/reshape | solution.py:470

commit v3 on v2

--- a/solution.py
+++ b/solution.py
@@ -261,30 +261,29 @@
                 suf_m[g, mine, :] = jnp.broadcast_to(state[0][rows_here] * scale, shape)
 
     suffix(0)
-    for j in range(2, pairs):
-        forward(j)
-    for s in range(1, own):
-        suffix(s)
 
     block = min(512, positions)
 
     def tile(j):
         mine, theirs = at_z(j, 0), at_z(j, 1)
 
+        stages = [(g, b) for g in range(groups) for b in range(positions // block)]
+        queries, tops, sums = {}, {}, {}
         for g in range(groups):
-            q = jnp.concatenate(
+            queries[g] = jnp.concatenate(
                 [qbuf[at, :, :, :, g].astype(F32).reshape(unit, head_dim) for at in (mine, theirs)],
                 axis=0).astype(BF16)
-            tops, sums = [], []
-            for b in range(positions // block):
-                here = slice(b * block, (b + 1) * block)
-                scores = dot_nt(keys[g, here, :], q)
-                top = jnp.max(scores, axis=0, keepdims=True)
-                weights = jnp.exp2((scores - top) * scale).astype(BF16)
-                tops.append(top * scale)
-                sums.append(dot(values_t[g, :, here], weights))
-            top = functools.reduce(jnp.maximum, tops)
-            total = sum(one * jnp.exp2(m - top) for one, m in zip(sums, tops))
+            tops[g], sums[g] = [], []
+
+        def score(g, b):
+            return dot_nt(keys[g, b * block:(b + 1) * block, :], queries[g])
+
+        def value(g, b, weights):
+            sums[g].append(dot(values_t[g, :, b * block:(b + 1) * block], weights))
+
+        def finish(g):
+            top = functools.reduce(jnp.maximum, tops[g])
+            total = sum(one * jnp.exp2(m - top) for one, m in zip(sums[g], tops[g]))
             stats = jnp.concatenate([
                 jnp.broadcast_to(top, (4, 2 * unit)), total[head_dim:head_dim + 4]], axis=0)
             total = total[:head_dim]
@@ -292,6 +291,21 @@
             own_s[j, g] = stats[:, :unit]
             xo_send[j, g] = total[:, unit:].astype(BF16)
             xs_send[j, g] = stats[:, unit:]
+
+        scores = score(*stages[0])
+        waiting = None
+        for i, (g, b) in enumerate(stages):
+            following = score(*stages[i + 1]) if i + 1 < len(stages) else None
+            if waiting is not None:
+                value(*waiting)
+            top = jnp.max(scores, axis=0, keepdims=True)
+            tops[g].append(top * scale)
+            waiting = (g, b, jnp.exp2((scores - top) * scale).astype(BF16))
+            scores = following
+            if b == 0 and g:
+                finish(g - 1)
+        value(*waiting)
+        finish(groups - 1)
 
     xs = {}
     zs = {}
@@ -338,11 +352,15 @@
 
     order = list(range(1, pairs)) + [0]
     for i, j in enumerate(order):
+        if j and j + 1 < pairs:
+            forward(j + 1)
         gx[j].wait_recv()
         tile(j)
         send_x(j)
         if i:
             merge_x(order[i - 1])
+    for s in range(1, own):
+        suffix(s)
     merge_x(0)
 
     for j in range(1, pairs):

time: 45.2 us -> 40.4 us (0.89)
  Pallas kernels: 41.9 us -> 37.1 us
    pallas_call x1, Pallas kernels: 41.9 us -> 37.1 us  [local(): pl.pallas_call(functools.partial(kernel, sizes), out_shape=jax.ShapeDtype...]
where the time goes in v3:
time: 40.4 us; the launch traced here: 40.1 us
  Pallas kernels  37.1 us (92%)
  local copies, waits for them, and re-layouts  3.01 us (7%)
    pallas_call x1, Pallas kernels, local(): pl.pallas_call(functools.partial(kernel, sizes), out_shape=jax.ShapeDtype...  37.1 us
    reshape x1, local copies, waits for them, and re-layouts, local(): queries.reshape(by_head)  1.53 us
    reshape x1, local copies, waits for them, and re-layouts, local(): return result.reshape(own, steps, features)  1.49 us

profile of v3, /device:TPU:0, one launch (start us, length us, event | category | flops | bytes accessed | tf_op | source)
XLA Modules:
  0.0 40.1 jit_solution(12906198927705141211)
XLA Ops:
  0.0 1.5 %reshape.24.q_ref = bf16[2,2,4,2,8,128]{5,4,3,2,1,0:T(8,128)(2,1)} reshape(bf16[2,2,8192]{2,1,0:T(2,128)(2,1)} %param.8) | data formatting | bytes 131072 | tf_op jit(solution)/shard_map/reshape | solution.py:479
  1.5 37.1 %shard_map.82 = bf16[2,2,4,2,8,128]{5,4,3,2,1,0:T(8,128)(2,1)} custom-call(bf16[2,2,4,2,8,128]{5,4,3,2,1,0:T(8,128)(2,1)} %reshape.24.q_ref, bf16[2,16,128]{2,1,0:T(8,128)(2,1)} %bitcast.12, bf16[2,16,128]{2,1,0:T(8,128)(2,1)} %bitcast.13, s32[2]{0:T(128)} %len_ref.1, bf16[4096,128]{1,0:T(8,128)(2,1)} %bitcast.10, bf16[4096,128]{1,0:T(8,128)(2,1)} %bitcast.11, ...), custom_call_target="tpu_custom_call" | custom-call | tf_op jit(solution)/shard_map/pallas_call | solution.py:430
  38.6 1.5 %reshape.31 = bf16[2,2,8192]{2,1,0:T(2,128)(2,1)} reshape(bf16[2,2,4,2,8,128]{5,4,3,2,1,0:T(8,128)(2,1)} %shard_map.82) | data formatting | bytes 131072 | tf_op jit(solution)/shard_map/reshape | solution.py:488

commit v4 on v3

--- a/solution.py
+++ b/solution.py
@@ -26,7 +26,7 @@
 
 def kernel(
     sizes,
-    q_ref,
+    q_flat,
     nk_ref,
     nv_ref,
     len_ref,
@@ -41,6 +41,7 @@
     sv,
     keys,
     values_t,
+    q_ref,
     qbuf,
     own_o,
     own_s,
@@ -107,6 +108,14 @@
     partners += [(at_z(0, 1), d)]
     for partner in partners:
         pl.semaphore_signal(barrier, inc=1, device_id=partner, device_id_type=MESH)
+    for s in range(own):
+        wide = q_flat[s].astype(F32)
+        for t in range(steps):
+            for h in range(kv_heads):
+                first = h * per_group
+                q_ref[s, t, h // groups, h % groups] = jnp.concatenate(
+                    [wide[t:t + 1, (first + i) * head_dim:(first + i + 1) * head_dim]
+                     for i in range(per_group)], axis=0).astype(BF16)
     pl.semaphore_wait(barrier, len(partners))
 
     def remote(src, dst, send_sem, recv_sem, target):
@@ -177,8 +186,6 @@
     prepare_all(prepare_values)
     values_t[:, head_dim:, :] = jnp.ones_like(values_t[:, head_dim:, :])
 
-    forward(1)
-
     chunk = min(512, suffix_rows // kv_heads) * kv_heads
     per_step = kv_heads * per_group
     q_rows = steps * per_step
@@ -199,16 +206,17 @@
             [folded[t * per_group:(t + 1) * per_group, g:g + 1]
              for t in range(steps) for g in range(kv_heads)], axis=0)
 
-    def suffix(s):
-        q = q_ref[s].astype(F32).reshape(q_rows, head_dim).astype(BF16)
-        length = len_ref[s]
-
-        def merge(left, right):
-            top = jnp.maximum(left[0], right[0])
-            a = jnp.exp2((left[0] - top) * scale)
-            b = jnp.exp2((right[0] - top) * scale)
-            return top, left[1] * a + right[1] * b, left[2] * a + right[2] * b
-
+    def suffix_query(s):
+        return q_ref[s].astype(F32).reshape(q_rows, head_dim).astype(BF16)
+
+    def suffix_merge(left, right):
+        top = jnp.maximum(left[0], right[0])
+        a = jnp.exp2((left[0] - top) * scale)
+        b = jnp.exp2((right[0] - top) * scale)
+        return top, left[1] * a + right[1] * b, left[2] * a + right[2] * b
+
+    def suffix_new(s):
+        q = suffix_query(s)
         new_rows = steps * kv_heads
         col = lax.broadcasted_iota(jnp.int32, (q_rows, new_rows), 1)
         row = lax.broadcasted_iota(jnp.int32, (q_rows, new_rows), 0)
@@ -216,40 +224,38 @@
         masked = jnp.where(seen, dot_nt(q, nk_ref[s]), MASKED_SCORE)
         top = jnp.max(masked, axis=1, keepdims=True)
         weights = jnp.exp2((masked - top) * scale).astype(BF16)
-        state = (top, jnp.sum(weights.astype(F32), axis=1, keepdims=True), dot(weights, nv_ref[s]))
-        loads[2 + 2 * s].wait()
-        loads[3 + 2 * s].wait()
-
-        def part(b, state):
-            here = pl.ds(pl.multiple_of(b * chunk, chunk), chunk)
-            scores = dot_nt(q, sk[s, here, :])
-            left = length - b * (chunk // kv_heads)
-            found = []
-            for k in range(chunk // head_dim):
-                lanes = slice(k * head_dim, (k + 1) * head_dim)
-                picked = []
-                for t in range(steps):
-                    base = t * per_step
-                    one = scores[base:base + per_group, lanes]
-                    for g in range(1, kv_heads):
-                        first = base + g * per_group
-                        one = jnp.where(hits[g], scores[first:first + per_group, lanes], one)
-                    picked.append(one)
-                visible = lane_place < left - k * (head_dim // kv_heads)
-                found.append(jnp.where(visible, jnp.concatenate(picked, axis=0), MASKED_SCORE))
-            top = jnp.maximum(around(jnp.maximum, functools.reduce(jnp.maximum, found)), FLOOR)
-            total = 0.0
-            spread = []
-            for one in found:
-                weights = jnp.exp2((one - top) * scale).astype(BF16).astype(F32)
-                total = total + weights
-                spread.append(jnp.concatenate(
-                    [jnp.where(hits[g], weights[t * per_group:(t + 1) * per_group], 0.0)
-                     for t in range(steps) for g in range(kv_heads)], axis=0).astype(BF16))
-            summed = dot(jnp.concatenate(spread, axis=1), sv[s, here, :])
-            return merge(state, (by_row(top), by_row(around(jnp.add, total)), summed))
-
-        state = lax.fori_loop(0, suffix_rows // chunk, part, state)
+        return top, jnp.sum(weights.astype(F32), axis=1, keepdims=True), dot(weights, nv_ref[s])
+
+    def suffix_part(s, b):
+        here = slice(b * chunk, (b + 1) * chunk)
+        scores = dot_nt(suffix_query(s), sk[s, here, :])
+        left = len_ref[s] - b * (chunk // kv_heads)
+        found = []
+        for k in range(chunk // head_dim):
+            lanes = slice(k * head_dim, (k + 1) * head_dim)
+            picked = []
+            for t in range(steps):
+                base = t * per_step
+                one = scores[base:base + per_group, lanes]
+                for g in range(1, kv_heads):
+                    first = base + g * per_group
+                    one = jnp.where(hits[g], scores[first:first + per_group, lanes], one)
+                picked.append(one)
+            visible = lane_place < left - k * (head_dim // kv_heads)
+            found.append(jnp.where(visible, jnp.concatenate(picked, axis=0), MASKED_SCORE))
+        top = jnp.maximum(around(jnp.maximum, functools.reduce(jnp.maximum, found)), FLOOR)
+        total = 0.0
+        spread = []
+        for one in found:
+            weights = jnp.exp2((one - top) * scale).astype(BF16).astype(F32)
+            total = total + weights
+            spread.append(jnp.concatenate(
+                [jnp.where(hits[g], weights[t * per_group:(t + 1) * per_group], 0.0)
+                 for t in range(steps) for g in range(kv_heads)], axis=0).astype(BF16))
+        summed = dot(jnp.concatenate(spread, axis=1), sv[s, here, :])
+        return by_row(top), by_row(around(jnp.add, total)), summed
+
+    def suffix_store(s, state):
         for t in range(steps):
             for g in range(kv_heads):
                 first = t * per_step + g * per_group
@@ -260,7 +266,22 @@
                 suf_l[g, mine, :] = jnp.broadcast_to(state[1][rows_here], shape)
                 suf_m[g, mine, :] = jnp.broadcast_to(state[0][rows_here] * scale, shape)
 
-    suffix(0)
+    suffix_blocks = suffix_rows // chunk
+    pieces = [(s, b) for s in range(own) for b in range(suffix_blocks)]
+    states = {}
+
+    def suffix(many):
+        for _ in range(min(many, len(pieces))):
+            s, b = pieces.pop(0)
+            if b == 0:
+                states[s] = suffix_new(s)
+                loads[2 + 2 * s].wait()
+                loads[3 + 2 * s].wait()
+            states[s] = suffix_merge(states[s], suffix_part(s, b))
+            if b == suffix_blocks - 1:
+                suffix_store(s, states[s])
+
+    suffix(max(1, len(pieces) - 3))
 
     block = min(512, positions)
 
@@ -350,18 +371,17 @@
             for copy in zs[j]:
                 copy.start()
 
-    order = list(range(1, pairs)) + [0]
-    for i, j in enumerate(order):
-        if j and j + 1 < pairs:
+    for j in range(pairs):
+        if j + 1 < pairs:
             forward(j + 1)
         gx[j].wait_recv()
         tile(j)
         send_x(j)
-        if i:
-            merge_x(order[i - 1])
-    for s in range(1, own):
-        suffix(s)
-    merge_x(0)
+        if j:
+            merge_x(j - 1)
+    suffix(1)
+    merge_x(pairs - 1)
+    suffix(1)
 
     for j in range(1, pairs):
         for copy in zs[j]:
@@ -369,7 +389,7 @@
     for g in range(groups):
         total, stats = merged([(own_o[0, g], own_s[0, g])]
                               + [(zo_recv[j, g], zs_recv[j, g]) for j in range(1, pairs)])
-        fo[g] = total.T
+        fo[g] = total.T.astype(BF16)
         fs[g] = stats
     ps = []
     for j in range(1, dec_n):
@@ -382,24 +402,27 @@
         copy.start()
     po_recv[d] = fo[:, own_rows, :]
     ps_recv[d] = fs[...]
+    suffix(len(pieces))
     for copy in ps:
         copy.wait_recv()
     flat = ps_recv[...].reshape(kv_heads * 8, unit)
     stat_rows[...] = flat.T
     picked = stat_rows[own_rows, :]
-    for a in range(dec_n):
-        for g in range(groups):
-            h = a * groups + g
-            top_p = picked[:, h * 8:h * 8 + 1]
-            sum_p = picked[:, h * 8 + 4:h * 8 + 5]
-            top = jnp.maximum(top_p, suf_m[h])
-            left = jnp.exp2(top_p - top)
-            right = jnp.exp2(suf_m[h] - top)
-            result = (po_recv[a, g] * left + suf_o[h] * right) / (sum_p * left + suf_l[h] * right)
-            for s in range(own):
-                for t in range(steps):
-                    first = (s * steps + t) * per_group
-                    out_ref[s, t, a, g] = result[first:first + per_group].astype(BF16)
+    results = []
+    for h in range(kv_heads):
+        top_p = picked[:, h * 8:h * 8 + 1]
+        sum_p = picked[:, h * 8 + 4:h * 8 + 5]
+        top = jnp.maximum(top_p, suf_m[h])
+        left = jnp.exp2(top_p - top)
+        right = jnp.exp2(suf_m[h] - top)
+        prompt = po_recv[h // groups, h % groups].astype(F32)
+        results.append((prompt * left + suf_o[h] * right) / (sum_p * left + suf_l[h] * right))
+    for s in range(own):
+        out_ref[s] = jnp.concatenate(
+            [jnp.concatenate(
+                [one[first:first + 1] for first in
+                 range(s * per_row + i, (s + 1) * per_row, per_group)], axis=0)
+             for one in results for i in range(per_group)], axis=1).astype(BF16)
 
     for copy in list(g2.values()) + list(gx.values()):
         copy.wait_send()
@@ -427,9 +450,9 @@
     dma = pltpu.SemaphoreType.DMA
     moved = (pairs, groups, head_dim, unit)
     noted = (pairs, groups, 8, unit)
-    result = pl.pallas_call(
+    return pl.pallas_call(
         functools.partial(kernel, sizes),
-        out_shape=jax.ShapeDtypeStruct(by_head, BF16),
+        out_shape=jax.ShapeDtypeStruct((own, steps, features), BF16),
         in_specs=[vmem, vmem, vmem, pl.BlockSpec(memory_space=pltpu.SMEM)] + [anywhere] * 4,
         out_specs=vmem,
         scratch_shapes=[
@@ -439,6 +462,7 @@
             pltpu.VMEM((own, suffix_rows, head_dim), BF16),
             pltpu.VMEM((groups, positions, head_dim), BF16),
             pltpu.VMEM((groups, head_dim + 16, positions), BF16),
+            pltpu.VMEM(by_head, BF16),
             pltpu.VMEM((ctx_n, dec_n, own, steps, groups, per_group, head_dim), BF16),
             pltpu.VMEM(moved, F32),
             pltpu.VMEM(noted, F32),
@@ -450,9 +474,9 @@
             pltpu.VMEM(noted, F32),
             pltpu.VMEM(moved, BF16),
             pltpu.VMEM(noted, F32),
-            pltpu.VMEM((groups, unit, head_dim), F32),
+            pltpu.VMEM((groups, unit, head_dim), BF16),
             pltpu.VMEM((groups, 8, unit), F32),
-            pltpu.VMEM((dec_n, groups, rows, head_dim), F32),
+            pltpu.VMEM((dec_n, groups, rows, head_dim), BF16),
             pltpu.VMEM((dec_n, groups, 8, unit), F32),
             pltpu.VMEM((unit, kv_heads * 8), F32),
             pltpu.VMEM((kv_heads, rows, head_dim), F32),
@@ -476,7 +500,7 @@
             collective_id=0, has_side_effects=True, vmem_limit_bytes=56 * 1024 * 1024
         ),
     )(
-        queries.reshape(by_head),
+        queries,
         new_keys.reshape(own, steps * kv_heads, head_dim),
         new_values.reshape(own, steps * kv_heads, head_dim),
         lengths,
@@ -485,8 +509,6 @@
         suffix_keys.reshape(own, suffix_rows, head_dim),
         suffix_values.reshape(own, suffix_rows, head_dim),
     )
-    return result.reshape(own, steps, features)
-
 
 def solution(mesh):
     return jax.shard_map(

time: 40.4 us -> 39.2 us (0.970)
  local copies, waits for them, and re-layouts: 3.01 us -> 1.52 us
    reshape x2 -> x0, local copies, waits for them, and re-layouts: 3.01 us -> none  [the longest x1 1.53 us: local(): queries.reshape(by_head)]
    unnamed x0 -> x1, local copies, waits for them, and re-layouts: none -> 1.52 us
    pallas_call x1, Pallas kernels: 37.1 us -> 37.5 us  [local(): pl.pallas_call(functools.partial(kernel, sizes), out_shape=jax.ShapeDtype...]
where the time goes in v4:
time: 39.2 us; the launch traced here: 39 us
  Pallas kernels  37.5 us (96%)
  local copies, waits for them, and re-layouts  1.52 us (4%)
    pallas_call x1, Pallas kernels, local(): pl.pallas_call(functools.partial(kernel, sizes), out_shape=jax.ShapeDtype...  37.5 us
    unnamed x1, local copies, waits for them, and re-layouts  1.52 us

profile of v4, /device:TPU:0, one launch (start us, length us, event | category | flops | bytes accessed | tf_op | source)
XLA Modules:
  0.0 39.0 jit_solution(10222994040246858176)
XLA Ops:
  0.0 37.5 %shard_map.82 = bf16[2,2,8192]{2,1,0:T(2,128)(2,1)} custom-call(bf16[2,2,8192]{2,1,0:T(2,128)(2,1)} %q_flat.1, bf16[2,16,128]{2,1,0:T(8,128)(2,1)} %bitcast.10, bf16[2,16,128]{2,1,0:T(8,128)(2,1)} %bitcast.11, s32[2]{0:T(128)} %len_ref.1, bf16[4096,128]{1,0:T(8,128)(2,1)} %bitcast.8, bf16[4096,128]{1,0:T(8,128)(2,1)} %bitcast.9, ...), custom_call_target="tpu_custom_call" | custom-call | tf_op jit(solution)/shard_map/pallas_call | solution.py:453
  37.5 1.5 %copy.10 = bf16[2,2,8192]{2,1,0:T(2,128)(2,1)} copy(bf16[2,2,8192]{2,1,0:T(2,128)(2,1)} %shard_map.82) | data formatting | bytes 131072

commit v5 on v4

--- a/solution.py
+++ b/solution.py
@@ -142,9 +142,10 @@
         for g in range(groups):
             values_t[g, :head_dim, there] = turned[:, g * span:(g + 1) * span]
 
-    def prepare_all(prepare):
-        count = positions * groups // 256
-        at_once = 8
+    at_once = min(8, positions * groups // 256)
+    prepare_steps = positions * groups // 256 // at_once
+
+    def prepare_all(prepare, first, last):
 
         def step(i, carry):
             for k in range(at_once):
@@ -153,7 +154,7 @@
                         pl.ds(pl.multiple_of(b * span, span), span))
             return carry
 
-        lax.fori_loop(0, count // at_once, step, 0)
+        lax.fori_loop(first, last, step, 0)
 
     own_rows = pl.ds(pl.multiple_of(d * rows, rows), rows)
     g1 = []
@@ -164,7 +165,7 @@
         g1.append(copy)
     qbuf[c, d] = q_ref[:, :, d]
     loads[0].wait()
-    prepare_all(prepare_keys)
+    prepare_all(prepare_keys, 0, prepare_steps // 2)
     for copy in g1:
         copy.wait()
     g2 = {}
@@ -183,7 +184,8 @@
     forward(0)
 
     loads[1].wait()
-    prepare_all(prepare_values)
+    prepare_all(prepare_keys, prepare_steps // 2, prepare_steps)
+    prepare_all(prepare_values, 0, prepare_steps)
     values_t[:, head_dim:, :] = jnp.ones_like(values_t[:, head_dim:, :])
 
     chunk = min(512, suffix_rows // kv_heads) * kv_heads

time: 39.2 us -> 39.7 us (1.013)
  Pallas kernels: 37.5 us -> 38 us
    pallas_call x1, Pallas kernels: 37.5 us -> 38 us  [local(): pl.pallas_call(functools.partial(kernel, sizes), out_shape=jax.ShapeDtype...]
where the time goes in v5:
time: 39.7 us; the launch traced here: 39.5 us
  Pallas kernels  38 us (96%)
  local copies, waits for them, and re-layouts  1.52 us (4%)
    pallas_call x1, Pallas kernels, local(): pl.pallas_call(functools.partial(kernel, sizes), out_shape=jax.ShapeDtype...  38 us
    unnamed x1, local copies, waits for them, and re-layouts  1.52 us

profile of v5, /device:TPU:0, one launch (start us, length us, event | category | flops | bytes accessed | tf_op | source)
XLA Modules:
  0.0 39.5 jit_solution(12014488865497451822)
XLA Ops:
  0.0 38.0 %shard_map.82 = bf16[2,2,8192]{2,1,0:T(2,128)(2,1)} custom-call(bf16[2,2,8192]{2,1,0:T(2,128)(2,1)} %q_flat.1, bf16[2,16,128]{2,1,0:T(8,128)(2,1)} %bitcast.10, bf16[2,16,128]{2,1,0:T(8,128)(2,1)} %bitcast.11, s32[2]{0:T(128)} %len_ref.1, bf16[4096,128]{1,0:T(8,128)(2,1)} %bitcast.8, bf16[4096,128]{1,0:T(8,128)(2,1)} %bitcast.9, ...), custom_call_target="tpu_custom_call" | custom-call | tf_op jit(solution)/shard_map/pallas_call | solution.py:455
  38.0 1.5 %copy.10 = bf16[2,2,8192]{2,1,0:T(2,128)(2,1)} copy(bf16[2,2,8192]{2,1,0:T(2,128)(2,1)} %shard_map.82) | data formatting | bytes 131072
